TPU v7x, 32 devices: a whole 2x2x4 slice. The times are simulated.
32 devices in a mesh: row: 16 (over z, y, x), col: 2 (over core).
Axes of the slice: x: 2, y: 2, z: 4, core: 2. Of those that a mesh axis runs over, the one named last changes fastest.
Arguments:
- queries: bfloat16 [16384, 1024], P(('row', 'col')), may hold values from -150 to 150
- keys: bfloat16 [16384, 128], P(('col', 'row')), may hold values from -6.1 to 6.1
- values: bfloat16 [16384, 128], P(('col', 'row')), may hold values from -6 to 6
- row_ptr: int32 [129], replicated, may hold values from 0 to 2048, as said below
- col_blocks: int32 [2048], replicated, may hold values from 0 to 127, as said below
- w_out: bfloat16 [1024, 8192], replicated, may hold values from -0.1875 to 0.1875
Outputs:
- projected: bfloat16 [16384, 8192], P(('row', 'col'))
Inputs may be any that keep to these rules, and one draw needn't show every extreme that they name: row_ptr[0] is 0 and row_ptr never falls; block-row b lists row_ptr[b+1] - row_ptr[b] blocks, 1 to 31; row_ptr[g * 8] = g * 8 * 16 for every g; in every group of 8 consecutive block-rows some block-row lists exactly 31 blocks. col_blocks[e] lies in key group e mod 2, that is between (e mod 2) * 64 and (e mod 2) * 64 + 63; the blocks listed for one block-row are distinct.
All inputs are finite; a program needn't handle non-finite values.
Results may differ from a plain program's by a relative error of at most 0.0055.
Values may be sent and summed in bfloat16 or wider, within the bound.
A program may use at most 192 MiB of HBM per device.

v0:
```python
import functools
import math

import jax
import jax.numpy as jnp
from jax import lax
from jax.experimental import pallas as pl
from jax.experimental.pallas import tpu as pltpu
from jax.sharding import PartitionSpec as P

HEAD_DIM = 128
BLOCK = 128
ONES = 16
CHUNK = 256
LOW = -1e30
RATE = HEAD_DIM ** (-0.5) * math.log2(math.e)
MESH = pl.DeviceIdType.MESH
VMEM_LIMIT = 50 * 1024 * 1024


def grid_of(chips):
    side = 1
    while 4 * (2 * side) ** 2 <= chips:
        side *= 2
    return chips // (side * side), side, side


def near(here, k, size):
    if size == 2:
        return 1 - here
    below, above = here, size - 1 - here
    room = jnp.minimum(below, above)
    side = jnp.where(above >= below, 1, -1)
    both = (k + 1) // 2 * (1 if k % 2 else -1)
    return here + side * jnp.where(k <= 2 * room, both, k - room)


def gather_kernel(sizes, q_ref, k_ref, v_ref, qo_ref, k_all, vt_all, vt, lsem, qsem, ssem, rsem):
    row, col = lax.axis_index("row"), lax.axis_index("col")
    zs, ys, xs = sizes
    here = (row // (ys * xs), row // xs % ys, row % xs)

    def number(place):
        return (place[0] * ys + place[1]) * xs + place[2]

    def beside(axis, step):
        there = list(here)
        there[axis] = here[axis] + step
        inside = jnp.logical_and(there[axis] >= 0, there[axis] < sizes[axis])
        return number(there), inside

    for block in range(v_ref.shape[0] // BLOCK):
        rows = slice(block * BLOCK, (block + 1) * BLOCK)
        vt[rows, :] = v_ref[rows, :].T

    barrier = pltpu.get_barrier_semaphore()
    greeted = 1
    for axis in range(3):
        for step in (-1, 1):
            there, inside = beside(axis, step)

            @pl.when(inside)
            def _():
                pl.semaphore_signal(barrier, inc=1, device_id=(there, col), device_id_type=MESH)

            greeted = greeted + jnp.where(inside, 1, 0)
    pl.semaphore_signal(barrier, inc=1, device_id=(row, 1 - col), device_id_type=MESH)
    pl.semaphore_wait(barrier, greeted)

    alls = (k_all, vt_all)
    owns = (k_ref, vt)
    orders = ((0, 2, 1), (0, 1, 2))
    sends = []

    def copy(piece, origin, source, slot, there):
        return pltpu.make_async_remote_copy(
            src_ref=source,
            dst_ref=alls[piece].at[origin],
            send_sem=ssem.at[piece, origin, slot],
            recv_sem=rsem.at[piece, origin],
            device_id=(there, col),
            device_id_type=MESH,
        )

    def send(piece, origin, source, axis, step, wanted=None):
        there, inside = beside(axis, step)
        if wanted is not None:
            inside = jnp.logical_and(inside, wanted)
        slot = axis * 2 + (step + 1) // 2

        @pl.when(inside)
        def _():
            copy(piece, origin, source, slot, there).start()

        sends.append((inside, piece, origin, source, slot, there))

    def arrive(piece, level, place):
        origin = number(place)
        landed = alls[piece].at[origin]
        copy(piece, origin, landed, 0, row).wait_recv()
        order = orders[piece]
        axis = order[level]
        if sizes[axis] > 2:
            send(piece, origin, landed, axis, 1, place[axis] < here[axis])
            send(piece, origin, landed, axis, -1, place[axis] > here[axis])
        for later in order[level + 1 :]:
            for step in (-1, 1):
                send(piece, origin, landed, later, step)

    to_other = pltpu.make_async_remote_copy(
        src_ref=q_ref,
        dst_ref=qo_ref,
        send_sem=qsem.at[0],
        recv_sem=qsem.at[1],
        device_id=(row, 1 - col),
        device_id_type=MESH,
    )
    for piece in range(2):
        for axis in orders[piece]:
            for step in (-1, 1):
                send(piece, row, owns[piece], axis, step)
    to_other.start()
    keeps = [
        pltpu.make_async_copy(owns[piece], alls[piece].at[row], lsem.at[piece])
        for piece in range(2)
    ]
    for keep in keeps:
        keep.start()

    def placed(piece, ks):
        place = list(here)
        for axis, k in zip(orders[piece], ks):
            if k:
                place[axis] = near(here[axis], k, sizes[axis])
        return place

    lengths = [[sizes[axis] for axis in order] for order in orders]
    for k in range(zs + 1):
        if 0 < k < zs:
            for piece in range(2):
                arrive(piece, 0, placed(piece, (k, 0, 0)))
        if k:
            for piece in range(2):
                for k2 in range(1, lengths[piece][1]):
                    arrive(piece, 1, placed(piece, (k - 1, k2, 0)))
    for k in range(zs):
        for piece in range(2):
            for k2 in range(lengths[piece][1]):
                for k3 in range(1, lengths[piece][2]):
                    arrive(piece, 2, placed(piece, (k, k2, k3)))
    for keep in keeps:
        keep.wait()
    to_other.wait()
    for inside, piece, origin, source, slot, there in sends:

        @pl.when(inside)
        def _():
            copy(piece, origin, source, slot, there).wait_send()


def gathered(queries, keys, values, chips):
    sizes = grid_of(chips)
    whole = jax.ShapeDtypeStruct((chips,) + keys.shape, keys.dtype)
    anywhere = pl.BlockSpec(memory_space=pl.ANY)
    return pl.pallas_call(
        functools.partial(gather_kernel, sizes),
        out_shape=(jax.ShapeDtypeStruct(queries.shape, queries.dtype), whole, whole),
        in_specs=[anywhere, anywhere, pl.BlockSpec(memory_space=pltpu.VMEM)],
        out_specs=(anywhere, anywhere, anywhere),
        scratch_shapes=[
            pltpu.VMEM(values.shape, values.dtype),
            pltpu.SemaphoreType.DMA((2,)),
            pltpu.SemaphoreType.DMA((2,)),
            pltpu.SemaphoreType.DMA((2, chips, 6)),
            pltpu.SemaphoreType.DMA((2, chips)),
        ],
        compiler_params=pltpu.CompilerParams(collective_id=0, has_side_effects=True),
        name="gather",
    )(queries, keys, values)


def attend_kernel(
    ptr_ref, cols_ref, other_ref, own_ref, k_ref, vt_ref,
    out_other, stat_other, out_own, stat_own,
    row_of, first_of, second_of, both_of, opens, closes, live_of,
    qt, scores_a, scores_b, acc, top,
):
    row, col = lax.axis_index("row"), lax.axis_index("col")
    half_rows = own_ref.shape[0] // BLOCK
    width = own_ref.shape[1]
    base = col * (k_ref.shape[0] // BLOCK)

    def list_row(i, n):
        half = jnp.where(i < half_rows, 1 - col, col)
        block_row = (row * 2 + half) * half_rows + i % half_rows
        begin, end = ptr_ref[block_row], ptr_ref[block_row + 1]
        first = begin + (begin + col) % 2
        count = jnp.maximum(end - first + 1, 0) // 2
        pairs = (count + 1) // 2

        def put(t, n):
            entry = first + 4 * t
            both = 2 * t + 1 < count
            row_of[n] = i
            first_of[n] = cols_ref[entry] - base
            second_of[n] = cols_ref[jnp.where(both, entry + 2, entry)] - base
            both_of[n] = jnp.where(both, 1.0, 0.0)
            live_of[n] = 1.0
            opens[n] = jnp.where(t == 0, 1, 0)
            closes[n] = jnp.where(t == pairs - 1, 1, 0)
            return n + 1

        return lax.fori_loop(0, pairs, put, n)

    number = lax.fori_loop(0, 2 * half_rows, list_row, 0)
    for more in range(2):
        row_of[number + more] = row_of[number - 1]
        first_of[number + more] = first_of[number - 1]
        second_of[number + more] = second_of[number - 1]
        both_of[number + more] = 0.0
        live_of[number + more] = 0.0
        opens[number + more] = 0
        closes[number + more] = 1

    for out, stat in ((out_other, stat_other), (out_own, stat_own)):
        for i in range(half_rows):
            out[i] = jnp.zeros((HEAD_DIM, width), out.dtype)
            stat[i] = jnp.concatenate(
                [jnp.full((1, width), LOW, jnp.float32), jnp.zeros((7, width), jnp.float32)], axis=0
            )
    for half, ref in enumerate((other_ref, own_ref)):
        for i in range(half_rows):
            for start in range(0, width, HEAD_DIM):
                head = slice(start, start + HEAD_DIM)
                qt[half * half_rows + i, :, head] = ref[i * BLOCK : (i + 1) * BLOCK, head].T
    acc[...] = jnp.zeros_like(acc)
    top[...] = jnp.full_like(top, LOW)

    def block_of(ref, block):
        return ref[pl.ds(pl.multiple_of(block * BLOCK, BLOCK), BLOCK), :]

    def keys_of(p):
        return jnp.concatenate(
            [block_of(k_ref, first_of[p]), block_of(k_ref, second_of[p])], axis=0
        )

    def score(p, keys, part, into):
        into[:, part] = jnp.dot(keys, qt[row_of[p], :, part], preferred_element_type=jnp.float32)

    def values_of(p):
        def one(block, weight):
            ones = jnp.ones((ONES, BLOCK), vt_ref.dtype)
            whole = jnp.concatenate([block_of(vt_ref, block), ones], axis=0)
            return whole * jnp.full(whole.shape, weight, jnp.float32).astype(whole.dtype)

        return jnp.concatenate(
            [one(first_of[p], live_of[p]), one(second_of[p], both_of[p])], axis=1
        )

    parts = [slice(start, start + CHUNK) for start in range(0, width, CHUNK)]

    def step(p, scores_now, scores_next):
        keys_next = keys_of(p + 1)
        values = values_of(p)
        fresh = jnp.full((1, CHUNK), opens[p], jnp.int32) == 1
        for part in parts:
            score(p + 1, keys_next, part, scores_next)
            scores = scores_now[:, part]
            old = jnp.where(fresh, LOW, top[:, part])
            new = jnp.maximum(old, jnp.max(scores, axis=0, keepdims=True))
            weights = jnp.exp2((scores - new) * RATE).astype(jnp.bfloat16)
            term = jnp.dot(values, weights, preferred_element_type=jnp.float32)
            acc[:, part] = acc[:, part] * jnp.exp2((old - new) * RATE) + term
            top[:, part] = new
        i = row_of[p]

        def finish(out, stat, at):
            out[at] = acc[:HEAD_DIM, :].astype(out.dtype)
            stat[at] = jnp.concatenate([top[...], acc[HEAD_DIM : HEAD_DIM + 7, :]], axis=0)

        @pl.when(jnp.logical_and(closes[p] == 1, i < half_rows))
        def _():
            finish(out_other, stat_other, i)

        @pl.when(jnp.logical_and(closes[p] == 1, i >= half_rows))
        def _():
            finish(out_own, stat_own, i - half_rows)

    keys = keys_of(0)
    for part in parts:
        score(0, keys, part, scores_a)

    def two(t, carry):
        step(2 * t, scores_a, scores_b)
        step(2 * t + 1, scores_b, scores_a)
        return carry

    lax.fori_loop(0, (number + 1) // 2, two, 0)


def attend(row_ptr, col_blocks, other, own, keys, values_t, entries):
    rows, width = own.shape[0] // BLOCK, own.shape[1]
    in_vmem = pl.BlockSpec(memory_space=pltpu.VMEM)
    in_smem = pl.BlockSpec(memory_space=pltpu.SMEM)
    listed = (entries + 2 * rows) // 2 + 4
    result = (
        jax.ShapeDtypeStruct((rows, HEAD_DIM, width), jnp.bfloat16),
        jax.ShapeDtypeStruct((rows, 8, width), jnp.float32),
    )
    return pl.pallas_call(
        attend_kernel,
        out_shape=result + result,
        in_specs=[in_smem, in_smem] + [in_vmem] * 4,
        out_specs=(in_vmem,) * 4,
        scratch_shapes=[pltpu.SMEM((listed,), jnp.int32)] * 3
        + [pltpu.SMEM((listed,), jnp.float32)]
        + [pltpu.SMEM((listed,), jnp.int32)] * 2
        + [
            pltpu.SMEM((listed,), jnp.float32),
            pltpu.VMEM((2 * rows, HEAD_DIM, width), jnp.bfloat16),
            pltpu.VMEM((2 * BLOCK, width), jnp.float32),
            pltpu.VMEM((2 * BLOCK, width), jnp.float32),
            pltpu.VMEM((HEAD_DIM + ONES, width), jnp.float32),
            pltpu.VMEM((1, width), jnp.float32),
        ],
        compiler_params=pltpu.CompilerParams(vmem_limit_bytes=VMEM_LIMIT),
        cost_estimate=pl.CostEstimate(
            flops=entries * 4 * BLOCK * width * HEAD_DIM,
            bytes_accessed=4 * keys.size,
            transcendentals=entries * BLOCK * width,
        ),
        name="attend",
    )(row_ptr, col_blocks, other, own, keys, values_t)


def project_kernel(out_a, stat_a, out_b, stat_b, w_ref, o_ref, attention):
    rows, _, width = out_a.shape

    @pl.when(pl.program_id(0) == 0)
    def _():
        for i in range(rows):
            max_a, max_b = stat_a[i, 0:1, :], stat_b[i, 0:1, :]
            peak = jnp.maximum(max_a, max_b)
            scale_a = jnp.exp2((max_a - peak) * RATE)
            scale_b = jnp.exp2((max_b - peak) * RATE)
            total = stat_a[i, 1:2, :] * scale_a + stat_b[i, 1:2, :] * scale_b
            scale_a, scale_b = scale_a / total, scale_b / total
            for start in range(0, width, HEAD_DIM):
                head = slice(start, start + HEAD_DIM)
                joined = (
                    out_a[i, :, head].astype(jnp.float32) * scale_a[:, head]
                    + out_b[i, :, head].astype(jnp.float32) * scale_b[:, head]
                )
                attention[i * BLOCK : (i + 1) * BLOCK, head] = joined.T.astype(attention.dtype)

    o_ref[...] = jnp.dot(
        attention[...], w_ref[...], preferred_element_type=jnp.float32
    ).astype(o_ref.dtype)


def project(own, other, w_out):
    rows, _, width = own[0].shape
    tokens, columns = rows * BLOCK, w_out.shape[1]
    tile = 1024
    partial = pl.BlockSpec(own[0].shape, lambda j: (0, 0, 0))
    stats = pl.BlockSpec(own[1].shape, lambda j: (0, 0, 0))
    return pl.pallas_call(
        project_kernel,
        out_shape=jax.ShapeDtypeStruct((tokens, columns), jnp.bfloat16),
        grid=(columns // tile,),
        in_specs=[
            partial,
            stats,
            partial,
            stats,
            pl.BlockSpec((width, tile), lambda j: (0, j)),
        ],
        out_specs=pl.BlockSpec((tokens, tile), lambda j: (0, j)),
        scratch_shapes=[pltpu.VMEM((tokens, width), jnp.bfloat16)],
        compiler_params=pltpu.CompilerParams(vmem_limit_bytes=VMEM_LIMIT),
        cost_estimate=pl.CostEstimate(
            flops=2 * tokens * width * columns,
            bytes_accessed=2 * (width * columns + tokens * columns),
            transcendentals=0,
        ),
        name="project",
    )(*own, *other, w_out)


def local(queries, keys, values, row_ptr, col_blocks, w_out):
    chips = lax.axis_size("row")
    other_queries, k_all, vt_all = gathered(queries, keys, values, chips)
    k_all = k_all.reshape(-1, HEAD_DIM)
    vt_all = vt_all.reshape(-1, BLOCK)
    entries = col_blocks.shape[0] // (chips * lax.axis_size("col"))
    results = attend(row_ptr, col_blocks, other_queries, queries, k_all, vt_all, entries)
    received = [lax.ppermute(part, "col", [(0, 1), (1, 0)]) for part in results[:2]]
    own = results[2:]
    return project(own, received, w_out)


def solution(mesh):
    in_specs = (
        P(("row", "col"), None),
        P(("col", "row"), None),
        P(("col", "row"), None),
        P(),
        P(),
        P(),
    )
    out_specs = P(("row", "col"), None)
    return jax.shard_map(local, mesh=mesh, in_specs=in_specs, out_specs=out_specs, check_vma=False)
```

profile of v0, /device:TPU:0, one launch (start us, length us, event | category | flops | bytes accessed | tf_op | source)
XLA Modules:
  0.0 83.8 jit_solution(10162077742047724690)
XLA Ops:
  0.0 43.0 %gather.1 = (bf16[512,1024]{1,0:T(8,128)(2,1)}, bf16[16,512,128]{2,1,0:T(8,128)(2,1)}, bf16[16,512,128]{2,1,0:T(8,128)(2,1)}) custom-call(bf16[512,1024]{1,0:T(8,128)(2,1)} %own_ref.1, bf16[512,128]{1,0:T(8,128)(2,1)} %k_ref.1, bf16[512,128]{1,0:T(8,128)(2,1)} %v_ref.1), custom_call_target="tpu_custom_call" | custom-call | tf_op jit(solution)/shard_map/gather/pallas_call | solution.py:165
  43.0 0.0 copy-start
  43.0 1.2 %copy-done = bf16[512,1024]{1,0:T(8,128)(2,1)S(1)} copy-done((bf16[512,1024]{1,0:T(8,128)(2,1)S(1)}, bf16[512,1024]{1,0:T(8,128)(2,1)}, u32[]{:S(2)}) %copy-start) | copy-done | bytes 1048600
  44.2 0.0 copy-start.1
  44.2 0.7 copy-done.1
  44.9 0.0 copy-start.2
  44.9 0.7 copy-done.2
  45.6 19.4 %attend.1 = (bf16[4,128,1024]{2,1,0:T(8,128)(2,1)S(1)}, f32[4,8,1024]{2,1,0:T(8,128)S(1)}, bf16[4,128,1024]{2,1,0:T(8,128)(2,1)S(1)}, f32[4,8,1024]{2,1,0:T(8,128)S(1)}) custom-call(s32[129]{0:T(256)S(1)} %copy-done.2, s32[2048]{0:T(1024)S(1)} %copy-done.1, bf16[512,1024]{1,0:T(8,128)(2,1)S(1)} %copy-done, bf16[512,1024]{1,0:T(8,128)(2,1)} %own_ref.1, ...), custom_call_target="tpu_custom_call" | custom-call | flops 4294967296 | bytes 4194304 | tf_op jit(solution)/shard_map/attend/pallas_call | solution.py:310
  65.1 0.1 collective-permute-start
  65.1 0.5 collective-permute-start.1
  65.6 2.3 %collective-permute-done.1.stat_b = f32[4,8,1024]{2,1,0:T(8,128)S(1)} collective-permute-done((f32[4,8,1024]{2,1,0:T(8,128)S(1)}, f32[4,8,1024]{2,1,0:T(8,128)S(1)}, u32[]{:S(2)}, u32[]{:S(2)}) %collective-permute-start.1) | collective-permute-done | bytes 131104 | tf_op jit(solution)/shard_map/ppermute | solution.py:397
  68.0 0.0 collective-permute-done.out_b
  68.0 15.8 %project.1 = bf16[512,8192]{1,0:T(8,128)(2,1)} custom-call(bf16[4,128,1024]{2,1,0:T(8,128)(2,1)S(1)} %get-tuple-element.15.out_a, f32[4,8,1024]{2,1,0:T(8,128)S(1)} %get-tuple-element.16.stat_a, bf16[4,128,1024]{2,1,0:T(8,128)(2,1)S(1)} %collective-permute-done.out_b, f32[4,8,1024]{2,1,0:T(8,128)S(1)} %collective-permute-done.1.stat_b, bf16[1024,8192]{1,0:T(8,128)(2,1)} %w_ref.1), custom_call_target="tpu_custom_call" | custom-call | flops 8589934592 | bytes 25165824 | tf_op jit(solution)/shard_map/project/pallas_call | solution.py:367
Async XLA Ops:
  43.0 1.2 %copy-start = (bf16[512,1024]{1,0:T(8,128)(2,1)S(1)}, bf16[512,1024]{1,0:T(8,128)(2,1)}, u32[]{:S(2)}) copy-start(bf16[512,1024]{1,0:T(8,128)(2,1)} %get-tuple-element.12.other_ref) | copy-start | bytes 3145732
  44.2 0.7 copy-start.1
  44.9 0.7 copy-start.2
  65.1 2.9 %collective-permute-start = (bf16[4,128,1024]{2,1,0:T(8,128)(2,1)S(1)}, bf16[4,128,1024]{2,1,0:T(8,128)(2,1)S(1)}, u32[]{:S(2)}, u32[]{:S(2)}) collective-permute-start(bf16[4,128,1024]{2,1,0:T(8,128)(2,1)S(1)} %get-tuple-element.17), channel_id=1, source_target_pairs={{0,1},{1,0},{2,3},{3,2},{4,5},{5,4},{6,7},{7,6},{8,9},{9,8},{10,11... | collective-permute-start | bytes 3145736 | tf_op jit(solution)/shard_map/ppermute | solution.py:397
  65.1 2.8 %collective-permute-start.1 = (f32[4,8,1024]{2,1,0:T(8,128)S(1)}, f32[4,8,1024]{2,1,0:T(8,128)S(1)}, u32[]{:S(2)}, u32[]{:S(2)}) collective-permute-start(f32[4,8,1024]{2,1,0:T(8,128)S(1)} %get-tuple-element.18), channel_id=1, source_target_pairs={{0,1},{1,0},{2,3},{3,2},{4,5},{5,4},{6,7},{7,6},{8,9},{9,8},{10,11... | collective-permute-start | bytes 393224 | tf_op jit(solution)/shard_map/ppermute | solution.py:397
where the time goes:
time: 84.2 us; the launch traced here: 83.8 us
  Pallas kernels  78.3 us (93%)
  local copies, waits for them, and re-layouts  2.59 us (3%)
  waiting for transfers between devices  2.34 us (3%)
    pallas_call x1, Pallas kernels, gathered(): pl.pallas_call(functools.partial(gather_kernel, sizes), out_shape=(jax.Sh...  43 us
    pallas_call x1, Pallas kernels, attend(): pl.pallas_call(attend_kernel, out_shape=result + result, in_specs=[in_sme...  19.4 us
    pallas_call x1, Pallas kernels, project(): pl.pallas_call(project_kernel, out_shape=jax.ShapeDtypeStruct((tokens, co...  15.8 us
    unnamed x6, local copies, waits for them, and re-layouts  2.59 us
    ppermute x2, waiting for transfers between devices, local(): lax.ppermute(part, 'col', [(0, 1), (1, 0)])  2.34 us
  transfers between devices with their start and end apart: 2, of which 1 were waited for; matrix products, arithmetic and copies ran while one was open for 0% of the time, Pallas kernels for 0%

commit v1 on v0

--- a/solution.py
+++ b/solution.py
@@ -35,10 +35,33 @@
     return here + side * jnp.where(k <= 2 * room, both, k - room)
 
 
-def gather_kernel(sizes, q_ref, k_ref, v_ref, qo_ref, k_all, vt_all, vt, lsem, qsem, ssem, rsem):
+def pieces_of(blocks):
+    quarter = blocks // 4
+    orders = ((0, 2), (0, 1), (0, 2, 1), (0, 1, 2))
+    return [(piece * quarter, quarter, order) for piece, order in enumerate(orders)]
+
+
+def place_in(piece, place, sizes):
+    z, y, x = place
+    if piece == 0:
+        return z * sizes[2] + x
+    if piece == 1:
+        return z * sizes[1] + y
+    return (z * sizes[1] + y) * sizes[2] + x
+
+
+def counts_of(sizes):
+    zs, ys, xs = sizes
+    return (zs * xs, zs * ys, zs * ys * xs, zs * ys * xs)
+
+
+def gather_kernel(
+    sizes, q_ref, k_ref, v_ref, qo_ref, all_0, all_1, all_2, all_3, mine, lsem, qsem, ssem, rsem
+):
     row, col = lax.axis_index("row"), lax.axis_index("col")
     zs, ys, xs = sizes
     here = (row // (ys * xs), row // xs % ys, row % xs)
+    pieces = pieces_of(k_ref.shape[0] // BLOCK)
 
     def number(place):
         return (place[0] * ys + place[1]) * xs + place[2]
@@ -49,9 +72,12 @@
         inside = jnp.logical_and(there[axis] >= 0, there[axis] < sizes[axis])
         return number(there), inside
 
-    for block in range(v_ref.shape[0] // BLOCK):
-        rows = slice(block * BLOCK, (block + 1) * BLOCK)
-        vt[rows, :] = v_ref[rows, :].T
+    for piece, (begin, count, _) in enumerate(pieces):
+        for block in range(count):
+            rows = slice((begin + block) * BLOCK, (begin + block + 1) * BLOCK)
+            at = 2 * block * BLOCK
+            mine[piece, at : at + BLOCK, :] = k_ref[rows, :]
+            mine[piece, at + BLOCK : at + 2 * BLOCK, :] = v_ref[rows, :].T
 
     barrier = pltpu.get_barrier_semaphore()
     greeted = 1
@@ -67,9 +93,8 @@
     pl.semaphore_signal(barrier, inc=1, device_id=(row, 1 - col), device_id_type=MESH)
     pl.semaphore_wait(barrier, greeted)
 
-    alls = (k_all, vt_all)
-    owns = (k_ref, vt)
-    orders = ((0, 2, 1), (0, 1, 2))
+    alls = (all_0, all_1, all_2, all_3)
+    orders = [order for _, _, order in pieces]
     sends = []
 
     def copy(piece, origin, source, slot, there):
@@ -95,7 +120,7 @@
         sends.append((inside, piece, origin, source, slot, there))
 
     def arrive(piece, level, place):
-        origin = number(place)
+        origin = place_in(piece, place, sizes)
         landed = alls[piece].at[origin]
         copy(piece, origin, landed, 0, row).wait_recv()
         order = orders[piece]
@@ -115,14 +140,17 @@
         device_id=(row, 1 - col),
         device_id_type=MESH,
     )
-    for piece in range(2):
+    every = range(len(pieces))
+    for piece in every:
         for axis in orders[piece]:
             for step in (-1, 1):
-                send(piece, row, owns[piece], axis, step)
+                send(piece, place_in(piece, here, sizes), mine.at[piece], axis, step)
     to_other.start()
     keeps = [
-        pltpu.make_async_copy(owns[piece], alls[piece].at[row], lsem.at[piece])
-        for piece in range(2)
+        pltpu.make_async_copy(
+            mine.at[piece], alls[piece].at[place_in(piece, here, sizes)], lsem.at[piece]
+        )
+        for piece in every
     ]
     for keep in keeps:
         keep.start()
@@ -137,17 +165,18 @@
     lengths = [[sizes[axis] for axis in order] for order in orders]
     for k in range(zs + 1):
         if 0 < k < zs:
-            for piece in range(2):
+            for piece in every:
                 arrive(piece, 0, placed(piece, (k, 0, 0)))
         if k:
-            for piece in range(2):
+            for piece in every:
                 for k2 in range(1, lengths[piece][1]):
                     arrive(piece, 1, placed(piece, (k - 1, k2, 0)))
     for k in range(zs):
-        for piece in range(2):
-            for k2 in range(lengths[piece][1]):
-                for k3 in range(1, lengths[piece][2]):
-                    arrive(piece, 2, placed(piece, (k, k2, k3)))
+        for piece in every:
+            if len(orders[piece]) > 2:
+                for k2 in range(lengths[piece][1]):
+                    for k3 in range(1, lengths[piece][2]):
+                        arrive(piece, 2, placed(piece, (k, k2, k3)))
     for keep in keeps:
         keep.wait()
     to_other.wait()
@@ -158,37 +187,116 @@
             copy(piece, origin, source, slot, there).wait_send()
 
 
-def gathered(queries, keys, values, chips):
-    sizes = grid_of(chips)
-    whole = jax.ShapeDtypeStruct((chips,) + keys.shape, keys.dtype)
+def gathered(queries, keys, values, sizes):
+    counts = counts_of(sizes)
+    pieces = len(counts)
+    rows = 2 * keys.shape[0] // pieces
     anywhere = pl.BlockSpec(memory_space=pl.ANY)
+    in_vmem = pl.BlockSpec(memory_space=pltpu.VMEM)
     return pl.pallas_call(
         functools.partial(gather_kernel, sizes),
-        out_shape=(jax.ShapeDtypeStruct(queries.shape, queries.dtype), whole, whole),
-        in_specs=[anywhere, anywhere, pl.BlockSpec(memory_space=pltpu.VMEM)],
-        out_specs=(anywhere, anywhere, anywhere),
+        out_shape=(jax.ShapeDtypeStruct(queries.shape, queries.dtype),)
+        + tuple(jax.ShapeDtypeStruct((count, rows, HEAD_DIM), keys.dtype) for count in counts),
+        in_specs=[anywhere, in_vmem, in_vmem],
+        out_specs=(anywhere,) * (1 + pieces),
         scratch_shapes=[
-            pltpu.VMEM(values.shape, values.dtype),
+            pltpu.VMEM((pieces, rows, HEAD_DIM), keys.dtype),
+            pltpu.SemaphoreType.DMA((pieces,)),
             pltpu.SemaphoreType.DMA((2,)),
-            pltpu.SemaphoreType.DMA((2,)),
-            pltpu.SemaphoreType.DMA((2, chips, 6)),
-            pltpu.SemaphoreType.DMA((2, chips)),
+            pltpu.SemaphoreType.DMA((pieces, counts[-1], 6)),
+            pltpu.SemaphoreType.DMA((pieces, counts[-1])),
         ],
         compiler_params=pltpu.CompilerParams(collective_id=0, has_side_effects=True),
         name="gather",
     )(queries, keys, values)
 
 
-def attend_kernel(
-    ptr_ref, cols_ref, other_ref, own_ref, k_ref, vt_ref,
-    out_other, stat_other, out_own, stat_own,
-    row_of, first_of, second_of, both_of, opens, closes, live_of,
-    qt, scores_a, scores_b, acc, top,
-):
+def shifted(part, sizes, axis):
+    zs, ys, xs = sizes
+    received = []
+    for k in range(1, sizes[axis]):
+        pairs = []
+        for z in range(zs):
+            for y in range(ys):
+                for x in range(xs):
+                    to = [z, y, x]
+                    to[axis] = (to[axis] + k) % sizes[axis]
+                    pairs.append(((z * ys + y) * xs + x, (to[0] * ys + to[1]) * xs + to[2]))
+        received.append(lax.ppermute(part, "row", pairs))
+    return received
+
+
+def attend_kernel(sizes, late, parts, ptr_ref, cols_ref, *refs):
+    blocks_in, refs = refs[:parts], refs[parts:]
+    if late:
+        states, refs = refs[:4], refs[4:]
+    else:
+        (other_ref, own_ref), refs = refs[:2], refs[2:]
+    if late:
+        qt_in, refs = refs[0], refs[1:]
+    outs, refs = refs[:4], refs[4:]
+    if not late:
+        qt_out, refs = refs[0], refs[1:]
+    row_of, first_of, second_of, both_of, opens, closes, live_of = refs[:7]
+    held, sems, scores_a, scores_b, acc, top = refs[7:]
+    qt = qt_in if late else qt_out
+    out_other, stat_other, out_own, stat_own = outs
+
     row, col = lax.axis_index("row"), lax.axis_index("col")
-    half_rows = own_ref.shape[0] // BLOCK
-    width = own_ref.shape[1]
-    base = col * (k_ref.shape[0] // BLOCK)
+    half_rows, _, width = out_own.shape
+    zs, ys, xs = sizes
+    shift = xs.bit_length() - 1
+    counts = counts_of(sizes)
+    quarter = blocks_in[0].shape[1] // (2 * BLOCK)
+    shard = 4 * quarter
+    base = col * (shard * counts[-1])
+    my_y, my_x = (row >> shift) & (ys - 1), row & (xs - 1)
+
+    copies = []
+    begin = 0
+    for index, ref in enumerate(blocks_in):
+        copies.append(
+            pltpu.make_async_copy(ref, held.at[pl.ds(begin, ref.shape[0])], sems.at[index])
+        )
+        begin += ref.shape[0]
+    for copy in copies:
+        copy.start()
+
+    def locate(block):
+        origin, within = lax.div(block, shard), lax.rem(block, shard)
+        piece, rest = lax.div(within, quarter), lax.rem(within, quarter)
+        x, y, z = origin & (xs - 1), (origin >> shift) & (ys - 1), origin >> (2 * shift)
+        is_0, is_1 = piece == 0, piece == 1
+        here_0, here_1 = z * xs + x, z * ys + y
+        if late:
+            back_y, back_x = (my_y - y) & (ys - 1), (my_x - x) & (xs - 1)
+            held_here = jnp.logical_or(
+                jnp.logical_and(is_0, back_y != 0), jnp.logical_and(is_1, back_x != 0)
+            )
+            place = jnp.where(
+                is_0,
+                (back_y - 1) * counts[0] + here_0,
+                ((ys - 1) + (back_x - 1)) * counts[0] + here_1,
+            )
+        else:
+            held_here = jnp.logical_or(
+                jnp.logical_or(piece >= 2, jnp.logical_and(is_0, y == my_y)),
+                jnp.logical_and(is_1, x == my_x),
+            )
+            place = jnp.where(
+                is_0,
+                here_0,
+                jnp.where(
+                    is_1,
+                    counts[0] + here_1,
+                    counts[0] + counts[1] + (piece - 2) * counts[2] + origin,
+                ),
+            )
+        return held_here, place * quarter + rest
+
+    row_of[0] = 0
+    first_of[0] = 0
+    second_of[0] = 0
 
     def list_row(i, n):
         half = jnp.where(i < half_rows, 1 - col, col)
@@ -196,52 +304,73 @@
         begin, end = ptr_ref[block_row], ptr_ref[block_row + 1]
         first = begin + (begin + col) % 2
         count = jnp.maximum(end - first + 1, 0) // 2
-        pairs = (count + 1) // 2
-
-        def put(t, n):
-            entry = first + 4 * t
-            both = 2 * t + 1 < count
-            row_of[n] = i
-            first_of[n] = cols_ref[entry] - base
-            second_of[n] = cols_ref[jnp.where(both, entry + 2, entry)] - base
-            both_of[n] = jnp.where(both, 1.0, 0.0)
-            live_of[n] = 1.0
-            opens[n] = jnp.where(t == 0, 1, 0)
-            closes[n] = jnp.where(t == pairs - 1, 1, 0)
-            return n + 1
-
-        return lax.fori_loop(0, pairs, put, n)
+
+        def put(t, k):
+            kept, place = locate(cols_ref[first + 2 * t] - base)
+            odd = k & 1
+            at = n + (k >> 1)
+            start = jnp.where(odd == 1, first_of[at], jnp.where(kept, place, 0))
+            first_of[at] = start
+            second_of[at] = jnp.where(kept, place, start)
+            both_of[at] = jnp.where(jnp.logical_and(kept, odd == 1), 1.0, 0.0)
+            live_of[at] = 1.0
+            row_of[at] = i
+            opens[at] = jnp.where(k < 2, 1, 0)
+            closes[at] = 0
+            return k + jnp.where(kept, 1, 0)
+
+        k = lax.fori_loop(0, count, put, 0)
+        n = n + ((k + 1) >> 1)
+
+        @pl.when(k > 0)
+        def _():
+            closes[n - 1] = 1
+
+        return n
 
     number = lax.fori_loop(0, 2 * half_rows, list_row, 0)
+    last = jnp.maximum(number - 1, 0)
     for more in range(2):
-        row_of[number + more] = row_of[number - 1]
-        first_of[number + more] = first_of[number - 1]
-        second_of[number + more] = second_of[number - 1]
+        row_of[number + more] = row_of[last]
+        first_of[number + more] = first_of[last]
+        second_of[number + more] = first_of[last]
         both_of[number + more] = 0.0
         live_of[number + more] = 0.0
         opens[number + more] = 0
         closes[number + more] = 1
 
-    for out, stat in ((out_other, stat_other), (out_own, stat_own)):
-        for i in range(half_rows):
-            out[i] = jnp.zeros((HEAD_DIM, width), out.dtype)
-            stat[i] = jnp.concatenate(
-                [jnp.full((1, width), LOW, jnp.float32), jnp.zeros((7, width), jnp.float32)], axis=0
-            )
-    for half, ref in enumerate((other_ref, own_ref)):
-        for i in range(half_rows):
-            for start in range(0, width, HEAD_DIM):
-                head = slice(start, start + HEAD_DIM)
-                qt[half * half_rows + i, :, head] = ref[i * BLOCK : (i + 1) * BLOCK, head].T
+    if late:
+        for out, state in zip(outs, states):
+            for i in range(half_rows):
+                out[i] = state[i]
+    else:
+        for out, stat in ((out_other, stat_other), (out_own, stat_own)):
+            for i in range(half_rows):
+                out[i] = jnp.zeros((HEAD_DIM, width), out.dtype)
+                stat[i] = jnp.concatenate(
+                    [jnp.full((1, width), LOW, jnp.float32), jnp.zeros((7, width), jnp.float32)],
+                    axis=0,
+                )
+        for half, ref in enumerate((other_ref, own_ref)):
+            for i in range(half_rows):
+                for start in range(0, width, HEAD_DIM):
+                    head = slice(start, start + HEAD_DIM)
+                    qt[half * half_rows + i, :, head] = ref[i * BLOCK : (i + 1) * BLOCK, head].T
     acc[...] = jnp.zeros_like(acc)
     top[...] = jnp.full_like(top, LOW)
-
-    def block_of(ref, block):
-        return ref[pl.ds(pl.multiple_of(block * BLOCK, BLOCK), BLOCK), :]
+    for copy in copies:
+        copy.wait()
+
+    def block_of(place, values):
+        if quarter == 1:
+            return held[place, BLOCK * values : BLOCK * (values + 1), :]
+        which, rest = lax.div(place, quarter), lax.rem(place, quarter)
+        start = pl.multiple_of((2 * rest + values) * BLOCK, BLOCK)
+        return held[which, pl.ds(start, BLOCK), :]
 
     def keys_of(p):
         return jnp.concatenate(
-            [block_of(k_ref, first_of[p]), block_of(k_ref, second_of[p])], axis=0
+            [block_of(first_of[p], 0), block_of(second_of[p], 0)], axis=0
         )
 
     def score(p, keys, part, into):
@@ -249,30 +378,45 @@
 
     def values_of(p):
         def one(block, weight):
-            ones = jnp.ones((ONES, BLOCK), vt_ref.dtype)
-            whole = jnp.concatenate([block_of(vt_ref, block), ones], axis=0)
+            ones = jnp.ones((ONES, BLOCK), held.dtype)
+            whole = jnp.concatenate([block_of(block, 1), ones], axis=0)
             return whole * jnp.full(whole.shape, weight, jnp.float32).astype(whole.dtype)
 
         return jnp.concatenate(
             [one(first_of[p], live_of[p]), one(second_of[p], both_of[p])], axis=1
         )
 
-    parts = [slice(start, start + CHUNK) for start in range(0, width, CHUNK)]
+    chunks = [slice(start, start + CHUNK) for start in range(0, width, CHUNK)]
 
     def step(p, scores_now, scores_next):
+        i = row_of[p]
+        if late:
+
+            def resume(out, stat, at):
+                acc[:HEAD_DIM, :] = out[at].astype(jnp.float32)
+                acc[HEAD_DIM:, :] = jnp.broadcast_to(stat[at, 1:2, :], (ONES, width))
+                top[...] = stat[at, 0:1, :]
+
+            @pl.when(jnp.logical_and(opens[p] == 1, i < half_rows))
+            def _():
+                resume(states[0], states[1], i)
+
+            @pl.when(jnp.logical_and(opens[p] == 1, i >= half_rows))
+            def _():
+                resume(states[2], states[3], i - half_rows)
+
         keys_next = keys_of(p + 1)
         values = values_of(p)
         fresh = jnp.full((1, CHUNK), opens[p], jnp.int32) == 1
-        for part in parts:
+        for part in chunks:
             score(p + 1, keys_next, part, scores_next)
             scores = scores_now[:, part]
-            old = jnp.where(fresh, LOW, top[:, part])
+            old = top[:, part] if late else jnp.where(fresh, LOW, top[:, part])
             new = jnp.maximum(old, jnp.max(scores, axis=0, keepdims=True))
             weights = jnp.exp2((scores - new) * RATE).astype(jnp.bfloat16)
             term = jnp.dot(values, weights, preferred_element_type=jnp.float32)
             acc[:, part] = acc[:, part] * jnp.exp2((old - new) * RATE) + term
             top[:, part] = new
-        i = row_of[p]
 
         def finish(out, stat, at):
             out[at] = acc[:HEAD_DIM, :].astype(out.dtype)
@@ -287,7 +431,7 @@
             finish(out_own, stat_own, i - half_rows)
 
     keys = keys_of(0)
-    for part in parts:
+    for part in chunks:
         score(0, keys, part, scores_a)
 
     def two(t, carry):
@@ -298,26 +442,32 @@
     lax.fori_loop(0, (number + 1) // 2, two, 0)
 
 
-def attend(row_ptr, col_blocks, other, own, keys, values_t, entries):
-    rows, width = own.shape[0] // BLOCK, own.shape[1]
+def attend(sizes, late, row_ptr, col_blocks, blocks, others, entries, rows):
+    width = others[-1].shape[-1]
+    anywhere = pl.BlockSpec(memory_space=pl.ANY)
     in_vmem = pl.BlockSpec(memory_space=pltpu.VMEM)
     in_smem = pl.BlockSpec(memory_space=pltpu.SMEM)
     listed = (entries + 2 * rows) // 2 + 4
     result = (
         jax.ShapeDtypeStruct((rows, HEAD_DIM, width), jnp.bfloat16),
         jax.ShapeDtypeStruct((rows, 8, width), jnp.float32),
-    )
+    ) * 2
+    if not late:
+        result += (jax.ShapeDtypeStruct((2 * rows, HEAD_DIM, width), jnp.bfloat16),)
+    held = sum(part.shape[0] for part in blocks)
+    share = entries // 4 if late else 3 * entries // 4
     return pl.pallas_call(
-        attend_kernel,
-        out_shape=result + result,
-        in_specs=[in_smem, in_smem] + [in_vmem] * 4,
-        out_specs=(in_vmem,) * 4,
+        functools.partial(attend_kernel, sizes, late, len(blocks)),
+        out_shape=result,
+        in_specs=[in_smem] * 2 + [anywhere] * len(blocks) + [in_vmem] * len(others),
+        out_specs=(in_vmem,) * len(result),
         scratch_shapes=[pltpu.SMEM((listed,), jnp.int32)] * 3
         + [pltpu.SMEM((listed,), jnp.float32)]
         + [pltpu.SMEM((listed,), jnp.int32)] * 2
         + [
             pltpu.SMEM((listed,), jnp.float32),
-            pltpu.VMEM((2 * rows, HEAD_DIM, width), jnp.bfloat16),
+            pltpu.VMEM((held,) + blocks[0].shape[1:], blocks[0].dtype),
+            pltpu.SemaphoreType.DMA((len(blocks),)),
             pltpu.VMEM((2 * BLOCK, width), jnp.float32),
             pltpu.VMEM((2 * BLOCK, width), jnp.float32),
             pltpu.VMEM((HEAD_DIM + ONES, width), jnp.float32),
@@ -325,12 +475,12 @@
         ],
         compiler_params=pltpu.CompilerParams(vmem_limit_bytes=VMEM_LIMIT),
         cost_estimate=pl.CostEstimate(
-            flops=entries * 4 * BLOCK * width * HEAD_DIM,
-            bytes_accessed=4 * keys.size,
-            transcendentals=entries * BLOCK * width,
+            flops=share * 4 * BLOCK * width * HEAD_DIM,
+            bytes_accessed=2 * held * blocks[0].shape[1] * HEAD_DIM,
+            transcendentals=share * BLOCK * width,
         ),
-        name="attend",
-    )(row_ptr, col_blocks, other, own, keys, values_t)
+        name="attend_late" if late else "attend_early",
+    )(row_ptr, col_blocks, *blocks, *others)
 
 
 def project_kernel(out_a, stat_a, out_b, stat_b, w_ref, o_ref, attention):
@@ -389,11 +539,15 @@
 
 def local(queries, keys, values, row_ptr, col_blocks, w_out):
     chips = lax.axis_size("row")
-    other_queries, k_all, vt_all = gathered(queries, keys, values, chips)
-    k_all = k_all.reshape(-1, HEAD_DIM)
-    vt_all = vt_all.reshape(-1, BLOCK)
+    sizes = grid_of(chips)
+    rows = queries.shape[0] // BLOCK
     entries = col_blocks.shape[0] // (chips * lax.axis_size("col"))
-    results = attend(row_ptr, col_blocks, other_queries, queries, k_all, vt_all, entries)
+    other_queries, *parts = gathered(queries, keys, values, sizes)
+    late = shifted(parts[0], sizes, 1) + shifted(parts[1], sizes, 2)
+    early = attend(
+        sizes, False, row_ptr, col_blocks, parts, (other_queries, queries), entries, rows
+    )
+    results = attend(sizes, True, row_ptr, col_blocks, late, early, entries, rows)
     received = [lax.ppermute(part, "col", [(0, 1), (1, 0)]) for part in results[:2]]
     own = results[2:]
     return project(own, received, w_out)

time: 84.2 us -> 90.6 us (1.076)
  local copies, waits for them, and re-layouts: 2.59 us -> 5.43 us
  Pallas kernels: 78.3 us -> 81.1 us
  starting transfers between devices: 0.57 us -> 1.67 us
    pallas_call x1 -> x2, Pallas kernels: 19.4 us -> 28.2 us  [attend(): pl.pallas_call(functools.partial(attend_kernel, sizes, late, len(blocks))...]
    pallas_call x1, Pallas kernels: 43 us -> 37.1 us  [gathered(): pl.pallas_call(functools.partial(gather_kernel, sizes), out_shape=(jax.Sh...]
    unnamed x6 -> x12, local copies, waits for them, and re-layouts: 2.59 us -> 5.43 us
    ppermute x0 -> x2, starting transfers between devices: none -> 1.11 us  [shifted(): received.append(lax.ppermute(part, 'row', pairs))]
  transfers between devices with their start and end apart: 2 -> 4, of which waited for: 1 -> 1; matrix products, arithmetic and copies ran while one was open for 0% -> 0% of each run, Pallas kernels for 0% -> 19%
where the time goes in v1:
time: 90.6 us
  Pallas kernels  81.1 us (90%)
  local copies, waits for them, and re-layouts  5.43 us (6%)
  waiting for transfers between devices  2.34 us (3%)
  starting transfers between devices  1.67 us (2%)
    pallas_call x1, Pallas kernels, gathered(): pl.pallas_call(functools.partial(gather_kernel, sizes), out_shape=(jax.Sh...  37.1 us
    pallas_call x2, Pallas kernels, attend(): pl.pallas_call(functools.partial(attend_kernel, sizes, late, len(blocks))...  28.2 us
    pallas_call x1, Pallas kernels, project(): pl.pallas_call(project_kernel, out_shape=jax.ShapeDtypeStruct((tokens, co...  15.8 us
    unnamed x12, local copies, waits for them, and re-layouts  5.43 us
    ppermute x2, waiting for transfers between devices, local(): lax.ppermute(part, 'col', [(0, 1), (1, 0)])  2.34 us
  transfers between devices with their start and end apart: 4, of which 1 were waited for; matrix products, arithmetic and copies ran while one was open for 0% of the time, Pallas kernels for 19%

profile of v1, /device:TPU:0, one launch (start us, length us, event | category | flops | bytes accessed | tf_op | source)
XLA Modules:
  0.0 90.6 jit_solution(10518856696204116139)
XLA Ops:
  0.0 37.1 %gather.1 = (bf16[512,1024]{1,0:T(8,128)(2,1)}, bf16[8,256,128]{2,1,0:T(8,128)(2,1)}, bf16[8,256,128]{2,1,0:T(8,128)(2,1)}, bf16[16,256,128]{2,1,0:T(8,128)(2,1)}, bf16[16,256,128]{2,1,0:T(8,128)(2,1)}) custom-call(bf16[512,1024]{1,0:T(8,128)(2,1)} %refs_5_.1, bf16[512,128]{1,0:T(8,128)(2,1)} %k_ref.1, bf16[512,128]{1,0:T(8,128)(2,1)} %v_ref.1), custom_call_target="tpu_custom_call" | custom-call | tf_op jit(solution)/shard_map/gather/pallas_call | solution.py:196
  37.1 0.6 collective-permute-start
  37.7 0.5 collective-permute-start.1
  38.2 0.0 copy-start.2
  38.2 0.7 copy-done.2
  38.9 0.0 copy-start.3
  38.9 0.7 copy-done.3
  39.6 0.0 copy-start.4
  39.6 1.0 %copy-done.4 = bf16[8,256,128]{2,1,0:T(8,128)(2,1)S(1)} copy-done((bf16[8,256,128]{2,1,0:T(8,128)(2,1)S(1)}, bf16[8,256,128]{2,1,0:T(8,128)(2,1)}, u32[]{:S(2)}) %copy-start.4) | copy-done | bytes 524312
  40.6 0.0 copy-start.5
  40.6 1.0 %copy-done.5 = bf16[8,256,128]{2,1,0:T(8,128)(2,1)S(1)} copy-done((bf16[8,256,128]{2,1,0:T(8,128)(2,1)S(1)}, bf16[8,256,128]{2,1,0:T(8,128)(2,1)}, u32[]{:S(2)}) %copy-start.5) | copy-done | bytes 524312
  41.7 17.5 %attend_early.1 = (bf16[4,128,1024]{2,1,0:T(8,128)(2,1)S(1)}, f32[4,8,1024]{2,1,0:T(8,128)S(1)}, bf16[4,128,1024]{2,1,0:T(8,128)(2,1)S(1)}, f32[4,8,1024]{2,1,0:T(8,128)S(1)}, bf16[8,128,1024]{2,1,0:T(8,128)(2,1)}) custom-call(s32[129]{0:T(256)S(1)} %copy-done.3, s32[2048]{0:T(1024)S(1)} %copy-done.2, bf16[8,256,128]{2,1,0:T(8,128)(2,1)S(1)} %copy-done.5, ...), custom_call_target="tpu_custom_call" | custom-call | flops 3221225472 | bytes 3145728 | tf_op jit(solution)/shard_map/attend_early/pallas_call | solution.py:459
  59.2 0.0 copy-start
  59.2 1.0 %copy-done = bf16[4,128,1024]{2,1,0:T(8,128)(2,1)} copy-done((bf16[4,128,1024]{2,1,0:T(8,128)(2,1)}, bf16[4,128,1024]{2,1,0:T(8,128)(2,1)S(1)}, u32[]{:S(2)}) %copy-start) | copy-done | bytes 1048600
  60.2 0.0 copy-start.1
  60.2 1.0 %copy-done.1 = bf16[4,128,1024]{2,1,0:T(8,128)(2,1)} copy-done((bf16[4,128,1024]{2,1,0:T(8,128)(2,1)}, bf16[4,128,1024]{2,1,0:T(8,128)(2,1)S(1)}, u32[]{:S(2)}) %copy-start.1) | copy-done | bytes 1048600
  61.2 0.0 collective-permute-done.refs_0_
  61.2 0.0 collective-permute-done.1.refs_1_
  61.2 10.7 %attend_late.1 = (bf16[4,128,1024]{2,1,0:T(8,128)(2,1)S(1)}, f32[4,8,1024]{2,1,0:T(8,128)S(1)}, bf16[4,128,1024]{2,1,0:T(8,128)(2,1)S(1)}, f32[4,8,1024]{2,1,0:T(8,128)S(1)}) custom-call(s32[129]{0:T(256)S(1)} %copy-done.3, s32[2048]{0:T(1024)S(1)} %copy-done.2, bf16[8,256,128]{2,1,0:T(8,128)(2,1)S(1)} %collective-permute-done.refs_0_, ...), custom_call_target="tpu_custom_call" | custom-call | flops 1073741824 | bytes 1048576 | tf_op jit(solution)/shard_map/attend_late/pallas_call | solution.py:459
  71.8 0.1 collective-permute-start.2
  71.9 0.5 collective-permute-start.3
  72.4 2.3 %collective-permute-done.3.stat_b = f32[4,8,1024]{2,1,0:T(8,128)S(1)} collective-permute-done((f32[4,8,1024]{2,1,0:T(8,128)S(1)}, f32[4,8,1024]{2,1,0:T(8,128)S(1)}, u32[]{:S(2)}, u32[]{:S(2)}) %collective-permute-start.3) | collective-permute-done | bytes 131104 | tf_op jit(solution)/shard_map/ppermute | solution.py:551
  74.7 0.0 collective-permute-done.2.out_b
  74.7 15.8 %project.1 = bf16[512,8192]{1,0:T(8,128)(2,1)} custom-call(bf16[4,128,1024]{2,1,0:T(8,128)(2,1)S(1)} %get-tuple-element.29.out_a, f32[4,8,1024]{2,1,0:T(8,128)S(1)} %get-tuple-element.30.stat_a, bf16[4,128,1024]{2,1,0:T(8,128)(2,1)S(1)} %collective-permute-done.2.out_b, f32[4,8,1024]{2,1,0:T(8,128)S(1)} %collective-permute-done.3.stat_b, ...), custom_call_target="tpu_custom_call" | custom-call | flops 8589934592 | bytes 25165824 | tf_op jit(solution)/shard_map/project/pallas_call | solution.py:517
Async XLA Ops:
  37.1 24.1 %collective-permute-start = (bf16[8,256,128]{2,1,0:T(8,128)(2,1)}, bf16[8,256,128]{2,1,0:T(8,128)(2,1)S(1)}, u32[]{:S(2)}, u32[]{:S(2)}) collective-permute-start(bf16[8,256,128]{2,1,0:T(8,128)(2,1)} %get-tuple-element.19.refs_0_), channel_id=1, source_target_pairs={{0,4},{2,6},{4,0},{6,2},{8,12},{10,14},{12,8},{14,10},{16,20},{18,... | collective-permute-start | bytes 1572872 | tf_op jit(solution)/shard_map/ppermute | solution.py:225
  37.7 23.5 %collective-permute-start.1 = (bf16[8,256,128]{2,1,0:T(8,128)(2,1)}, bf16[8,256,128]{2,1,0:T(8,128)(2,1)S(1)}, u32[]{:S(2)}, u32[]{:S(2)}) collective-permute-start(bf16[8,256,128]{2,1,0:T(8,128)(2,1)} %get-tuple-element.20.refs_1_), channel_id=1, source_target_pairs={{0,2},{2,0},{4,6},{6,4},{8,10},{10,8},{12,14},{14,12},{16,18},{18,... | collective-permute-start | bytes 1572872 | tf_op jit(solution)/shard_map/ppermute | solution.py:225
  38.2 0.7 copy-start.2
  38.9 0.7 copy-start.3
  39.6 1.0 %copy-start.4 = (bf16[8,256,128]{2,1,0:T(8,128)(2,1)S(1)}, bf16[8,256,128]{2,1,0:T(8,128)(2,1)}, u32[]{:S(2)}) copy-start(bf16[8,256,128]{2,1,0:T(8,128)(2,1)} %get-tuple-element.20.refs_1_) | copy-start | bytes 1572868
  40.6 1.0 %copy-start.5 = (bf16[8,256,128]{2,1,0:T(8,128)(2,1)S(1)}, bf16[8,256,128]{2,1,0:T(8,128)(2,1)}, u32[]{:S(2)}) copy-start(bf16[8,256,128]{2,1,0:T(8,128)(2,1)} %get-tuple-element.19.refs_0_) | copy-start | bytes 1572868
  59.2 1.0 %copy-start = (bf16[4,128,1024]{2,1,0:T(8,128)(2,1)}, bf16[4,128,1024]{2,1,0:T(8,128)(2,1)S(1)}, u32[]{:S(2)}) copy-start(bf16[4,128,1024]{2,1,0:T(8,128)(2,1)S(1)} %get-tuple-element.24.refs_2_) | copy-start | bytes 3145732
  60.2 1.0 %copy-start.1 = (bf16[4,128,1024]{2,1,0:T(8,128)(2,1)}, bf16[4,128,1024]{2,1,0:T(8,128)(2,1)S(1)}, u32[]{:S(2)}) copy-start(bf16[4,128,1024]{2,1,0:T(8,128)(2,1)S(1)} %get-tuple-element.26.refs_4_) | copy-start | bytes 3145732
  71.8 2.9 %collective-permute-start.2 = (bf16[4,128,1024]{2,1,0:T(8,128)(2,1)S(1)}, bf16[4,128,1024]{2,1,0:T(8,128)(2,1)S(1)}, u32[]{:S(2)}, u32[]{:S(2)}) collective-permute-start(bf16[4,128,1024]{2,1,0:T(8,128)(2,1)S(1)} %get-tuple-element.31), channel_id=1, source_target_pairs={{0,1},{1,0},{2,3},{3,2},{4,5},{5,4},{6,7},{7,6},{8,9},{9,8},{10,11... | collective-permute-start | bytes 3145736 | tf_op jit(solution)/shard_map/ppermute | solution.py:551
  71.9 2.8 %collective-permute-start.3 = (f32[4,8,1024]{2,1,0:T(8,128)S(1)}, f32[4,8,1024]{2,1,0:T(8,128)S(1)}, u32[]{:S(2)}, u32[]{:S(2)}) collective-permute-start(f32[4,8,1024]{2,1,0:T(8,128)S(1)} %get-tuple-element.32), channel_id=1, source_target_pairs={{0,1},{1,0},{2,3},{3,2},{4,5},{5,4},{6,7},{7,6},{8,9},{9,8},{10,11... | collective-permute-start | bytes 393224 | tf_op jit(solution)/shard_map/ppermute | solution.py:551
